TPU v7x, 32 devices: a whole 2x2x4 slice. The times are simulated.
32 devices in a mesh: dp: 2 (over x), expert: 16 (over z, y, core).
Axes of the slice: x: 2, y: 2, z: 4, core: 2. Of those that a mesh axis runs over, the one named last changes fastest.
Arguments:
- routes: int32 [2048, 8], P('expert'), may hold values from 0 to 15, all different within a row; in each aligned block of 128 rows (0 to 127, 128 to 255, ...) at most 80 rows name the same one
- gates: float32 [2048, 8], P('expert'), may hold values from 0.1 to 1
- hidden: bfloat16 [16, 1280, 1024], P('expert', None, 'dp'), may hold values from -6 to 6
- w_down: bfloat16 [16, 1024, 7168], P('expert', None, 'dp'), may hold values from -0.25 to 0.25
- out_grad: bfloat16 [2048, 7168], P('expert', 'dp'), may hold values from -1.5 to 1.5
Outputs:
- mixed: bfloat16 [2048, 7168], P('expert', 'dp')
- hidden_grad: bfloat16 [16, 1280, 1024], P('expert', None, 'dp')
- weight_grad: bfloat16 [16, 1024, 7168], P('expert', None, 'dp')
- gate_grad: float32 [2048, 8], P('expert')
Inputs may be any that keep to these rules, and one draw needn't show every extreme that they name: `routes`: each token names 8 different experts; among the 128 tokens held by one device of the expert axis no expert is named more than 80 times, and in every draw some expert is named exactly 80 times by them.
All inputs are finite; a program needn't handle non-finite values.
Results may differ from a plain program's by a relative error of at most 0.014.
Values may be sent and summed in bfloat16 or wider, within the bound.
A program may use at most 128 MiB of HBM per device.

v0:
```python
import jax
import jax.numpy as jnp
from jax import lax
from jax.sharding import PartitionSpec as P


def per_device(routes, gates, hidden, w_down, out_grad):
    experts = lax.axis_size("expert")
    h_local = hidden[0]
    w_local = w_down[0]
    slots = h_local.shape[0]
    cap = slots // experts
    width = w_local.shape[1]
    tok_dev = routes.shape[0]
    topk = routes.shape[1]
    flat = routes.reshape(-1)
    onehot = (flat[:, None] == jnp.arange(experts, dtype=jnp.int32)[None, :]).astype(jnp.int32)
    before = jnp.cumsum(onehot, axis=0) - onehot
    rank = jnp.sum(before * onehot, axis=1)
    target = flat * cap + rank
    grad_wide = out_grad.astype(jnp.float32)
    send_grad = (
        (gates[:, :, None] * grad_wide[:, None, :])
        .astype(jnp.bfloat16)
        .reshape(tok_dev * topk, width)
    )
    grad_buffer = jnp.zeros((experts * cap, width), jnp.bfloat16).at[target].set(send_grad)
    grad_buffer = grad_buffer.reshape(experts, cap, width)
    whole = lax.all_gather(h_local, "dp", axis=1, tiled=True)
    expert_out = jnp.dot(whole, w_local, preferred_element_type=jnp.float32).astype(jnp.bfloat16)
    out_blocks = expert_out.reshape(experts, cap, width)
    returned, arrived = (
        lax.all_to_all(out_blocks, "expert", split_axis=0, concat_axis=0, tiled=True),
        lax.all_to_all(grad_buffer, "expert", split_axis=0, concat_axis=0, tiled=True),
    )
    rows = jnp.take(returned.reshape(experts * cap, width), target, axis=0)
    rows_wide = rows.reshape(tok_dev, topk, width).astype(jnp.float32)
    mixed = jnp.sum(gates[:, :, None] * rows_wide, axis=1).astype(jnp.bfloat16)
    partial_dots = jnp.sum(grad_wide[:, None, :] * rows_wide, axis=2)
    gate_grad = lax.psum(partial_dots, "dp")
    grad_slots = arrived.reshape(slots, width)
    weight_grad = lax.dot_general(
        whole, grad_slots, (((0,), (0,)), ((), ())), preferred_element_type=jnp.float32
    ).astype(jnp.bfloat16)
    partial_hidden = lax.dot_general(
        grad_slots, w_local, (((1,), (1,)), ((), ())), preferred_element_type=jnp.float32
    )
    hidden_grad = lax.psum_scatter(
        partial_hidden.astype(jnp.bfloat16), "dp", scatter_dimension=1, tiled=True
    )
    return (mixed, hidden_grad[None], weight_grad[None], gate_grad)


def solution(mesh):
    in_specs = (
        P("expert", None),
        P("expert", None),
        P("expert", None, "dp"),
        P("expert", None, "dp"),
        P("expert", "dp"),
    )
    out_specs = (
        P("expert", "dp"),
        P("expert", None, "dp"),
        P("expert", None, "dp"),
        P("expert", None),
    )
    return jax.shard_map(
        per_device, mesh=mesh, in_specs=in_specs, out_specs=out_specs, check_vma=False
    )
```

profile of v0, /device:TPU:16, one launch (start us, length us, event | category | flops | bytes accessed | tf_op | source)
XLA Modules:
  0.0 494.2 jit_solution(469519492268890451)
XLA Ops:
  7.2 0.8 copy.15
  8.0 0.1 eq.26
  8.0 0.1 reshape.101
  8.2 4.5 reduce-window.6
  12.7 0.1 slice.10
  12.8 0.1 copy.18
  12.9 0.1 copy.19
  13.0 0.1 broadcast_add_fusion
  13.1 0.1 mul.61
  13.2 1.4 convert_element_type.42
  14.6 0.8 copy.14
  15.3 0.1 mul.63
  15.5 15.6 %scatter_custom_fusion = bf16[1280,3584]{1,0:T(8,128)(2,1)} fusion(s32[1024]{0:T(1024)S(1)} %bitcast.60, f32[128,3584]{1,0:T(8,128)S(1)} %convert_element_type.42, f32[1024]{0:T(1024)S(1)} %mul.63, bf16[]{:T(256)} %constant.28.clone.1), kind=kCustom, calls=%fused_computation.9 | custom fusion | flops 7340032 | bytes 11014146 | tf_op jit(solution)/shard_map/scatter | solution.py:27
  31.1 6.2 %all-to-all-start.1 = ((bf16[16,80,3584]{2,1,0:T(8,128)(2,1)}), bf16[16,80,3584]{2,1,0:T(8,128)(2,1)}, u32[]{:S(2)}, u32[]{:S(2)}) async-start(bf16[16,80,3584]{2,1,0:T(8,128)(2,1)} %bitcast.55), calls=%async_computation.1 | async-start | bytes 18350080 | tf_op jit(solution)/shard_map/all_to_all | solution.py:34
  37.3 0.2 all-gather.3.cloned.1.call-start
  37.5 0.5 all-gather.3.cloned.1.call-update
  38.0 41.6 %all-gather.3.cloned.1.call-done = bf16[1,1280,1024]{2,1,0:T(8,128)(2,1)} async-done(((bf16[1,1280,512]{2,1,0:T(8,128)(2,1)}), bf16[1,1280,1024]{2,1,0:T(8,128)(2,1)}) %all-gather.3.cloned.1.call-update) | async-done | bytes 2621456 | tf_op jit(solution)/shard_map/all_gather | solution.py:29
  79.6 14.9 %convolution_convert_fusion = bf16[1280,3584]{1,0:T(8,128)(2,1)} fusion(bf16[1,1024,3584]{2,1,0:T(8,128)(2,1)} %param.8, bf16[1,1280,1024]{2,1,0:T(8,128)(2,1)} %all-gather.3.cloned.1.call-done), kind=kOutput, calls=%fused_computation.4 | convolution fusion | flops 9399828480 | bytes 19136512 | tf_op jit(solution)/shard_map/dot_general | solution.py:30
  94.5 142.2 %all-to-all-done.1 = bf16[16,80,3584]{2,1,0:T(8,128)(2,1)} async-done(((bf16[16,80,3584]{2,1,0:T(8,128)(2,1)}), bf16[16,80,3584]{2,1,0:T(8,128)(2,1)}, u32[]{:S(2)}, u32[]{:S(2)}) %all-to-all-start.1) | async-done | bytes 9175072 | tf_op jit(solution)/shard_map/all_to_all | solution.py:34
  236.7 4.7 all-to-all-start
  241.4 0.0 reduce-scatter.2.cloned.1.call-start
  241.5 15.4 %fusion.11 = bf16[1280,1024]{1,0:T(8,128)(2,1)} fusion(bf16[1280,3584]{1,0:T(8,128)(2,1)} %bitcast.11, bf16[1,1024,3584]{2,1,0:T(8,128)(2,1)} %param.8), kind=kOutput, calls=%fused_computation.18 | convolution fusion | flops 9396551680 | bytes 19136512 | tf_op jit(solution)/shard_map/dot_general | solution.py:45
  256.9 0.0 reduce-scatter.2.cloned.1.call-update
  256.9 0.1 reduce_sum.34
  257.0 0.1 broadcast_in_dim.36
  257.1 14.9 %fusion.9 = bf16[1,1024,3584]{1,2,0:T(8,128)(2,1)} fusion(bf16[1280,3584]{1,0:T(8,128)(2,1)} %bitcast.11, bf16[1,1280,1024]{2,1,0:T(8,128)(2,1)} %all-gather.3.cloned.1.call-done), kind=kOutput, calls=%fused_computation.16 | convolution fusion | flops 9398910976 | bytes 19136512 | tf_op jit(solution)/shard_map/dot_general | solution.py:42
  272.0 9.9 %copy.21 = bf16[1,1024,3584]{2,1,0:T(8,128)(2,1)} copy(bf16[1,1024,3584]{1,2,0:T(8,128)(2,1)} %fusion.9) | data formatting | bytes 14680064
  282.0 158.9 %all-to-all-done = bf16[16,80,3584]{2,1,0:T(8,128)(2,1)} async-done(((bf16[16,80,3584]{2,1,0:T(8,128)(2,1)}), bf16[16,80,3584]{2,1,0:T(8,128)(2,1)}, u32[]{:S(2)}, u32[]{:S(2)}) %all-to-all-start) | async-done | bytes 9175072 | tf_op jit(solution)/shard_map/all_to_all | solution.py:33
  440.8 18.6 %gather_fusion = bf16[1024,3584]{1,0:T(8,128)(2,1)} fusion(bf16[1280,3584]{1,0:T(8,128)(2,1)} %bitcast.5, s32[1024]{0:T(1024)S(1)} %broadcast_clamp_fusion), kind=kCustom, calls=%fused_computation | custom fusion | bytes 14684160 | tf_op jit(solution)/shard_map/jit(_take)/gather | solution.py:36
  459.4 5.1 %fusion.1 = f32[1024]{0:T(1024)S(1)} fusion(bf16[1024,3584]{1,0:T(8,128)(2,1)} %gather_fusion, f32[128,3584]{1,0:T(8,128)S(1)} %convert_element_type.42, pred[1024]{0:T(1024)(128)(4,1)S(1)} %broadcast_in_dim.36), kind=kLoop, calls=%fused_computation.6 | loop fusion | flops 14679040 | bytes 9180160 | tf_op jit(solution)/shard_map/reduce_sum | solution.py:39
  464.5 0.1 reduce_sum.38
  464.6 9.2 %psum.7 = f32[128,8]{1,0:T(8,128)S(1)} all-reduce(f32[128,8]{1,0:T(8,128)S(1)} %reduce_sum.38), channel_id=1, replica_groups=mesh['dp'=2,'expert'=16] {'dp'}, use_global_device_ids=true, to_apply=%region_7.8 | all-reduce | flops 1024 | bytes 8192 | tf_op jit(solution)/shard_map/psum | solution.py:40
  473.8 0.7 copy.22
  474.5 12.9 %multiply_reduce_fusion = bf16[128,3584]{1,0:T(8,128)(2,1)} fusion(bf16[1024,3584]{1,0:T(8,128)(2,1)} %gather_fusion, f32[128,8]{1,0:T(8,128)S(1)} %copy.14, pred[128,8]{1,0:T(8,128)(4,1)S(1)} %compare_and_fusion), kind=kLoop, calls=%fused_computation.7 | loop fusion | flops 14221312 | bytes 8262656 | tf_op jit(solution)/shard_map/reduce_sum | solution.py:38
  487.4 0.0 reduce-scatter.2.cloned.1.call-done
  (8 shorter events, 0.1 us)
Async XLA Ops:
  31.1 205.6 %all-to-all-start.1 = ((bf16[16,80,3584]{2,1,0:T(8,128)(2,1)}), bf16[16,80,3584]{2,1,0:T(8,128)(2,1)}, u32[]{:S(2)}, u32[]{:S(2)}) async-start(bf16[16,80,3584]{2,1,0:T(8,128)(2,1)} %bitcast.55), calls=%async_computation.1 | async-start | bytes 18350080 | tf_op jit(solution)/shard_map/all_to_all | solution.py:34
  37.3 42.3 %all-gather.3.cloned.1.call-start = ((), (), s32[]{:S(2)}) async-start(), calls=%async_computation.4 | async-start | bytes 3932160 | tf_op jit(solution)/shard_map/all_gather | solution.py:29
  236.7 204.1 %all-to-all-start = ((bf16[16,80,3584]{2,1,0:T(8,128)(2,1)}), bf16[16,80,3584]{2,1,0:T(8,128)(2,1)}, u32[]{:S(2)}, u32[]{:S(2)}) async-start(bf16[16,80,3584]{2,1,0:T(8,128)(2,1)} %bitcast.56), calls=%async_computation | async-start | bytes 18350080 | tf_op jit(solution)/shard_map/all_to_all | solution.py:33
  241.4 246.0 %reduce-scatter.2.cloned.1.call-start = ((), (), s32[]{:S(2)}) async-start(), calls=%async_computation.3 | async-start | bytes 3932160 | tf_op jit(solution)/shard_map/reduce_scatter | solution.py:48
Sparse Core Ops, SparseCore 0:
  39.7 39.9 all-gather.2
  257.0 38.4 reduce-scatter.1
where the time goes:
time: 495 us; the launch traced here: 494 us
  waiting for transfers between devices  343 us (69%)
  matrix products  45.2 us (9%)
  other arithmetic  39.7 us (8%)
  local copies, waits for them, and re-layouts  31.7 us (6%)
  between operations  14.1 us (3%)
  starting transfers between devices  11.1 us (2%)
  blocking collectives  9.16 us (2%)
    all_to_all x1, waiting for transfers between devices, per_device(): lax.all_to_all(out_blocks, 'expert', split_axis=0, concat_axis=0, tiled=T...  159 us
    all_to_all x1, waiting for transfers between devices, per_device(): lax.all_to_all(grad_buffer, 'expert', split_axis=0, concat_axis=0, tiled=...  142 us
    all_gather x1, waiting for transfers between devices, per_device(): whole = lax.all_gather(h_local, 'dp', axis=1, tiled=True)  41.6 us
    gather x1, local copies, waits for them, and re-layouts, per_device(): rows = jnp.take(returned.reshape(experts * cap, width), target, axis=0)  18.6 us
    scatter x1, other arithmetic, per_device(): jnp.zeros((experts * cap, width), jnp.bfloat16).at[target].set(send_grad)  15.6 us
    dot_general x1, matrix products, per_device(): lax.dot_general(grad_slots, w_local, (((1,), (1,)), ((), ())), preferred_...  15.4 us
    dot_general x1, matrix products, per_device(): lax.dot_general(whole, grad_slots, (((0,), (0,)), ((), ())), preferred_el...  14.9 us
    dot_general x1, matrix products, per_device(): jnp.dot(whole, w_local, preferred_element_type=jnp.float32)  14.9 us
  transfers between devices with their start and end apart: 4, of which 3 were waited for; matrix products, arithmetic and copies ran while one was open for 19% of the time, Pallas kernels for 0%

commit v1 on v0

v1 whole, which is shorter than its diff:
```python
import jax
import jax.numpy as jnp
from jax import lax
from jax.sharding import PartitionSpec as P

CHUNKS = 2


def swap(x):
    return lax.ppermute(x, "dp", [(0, 1), (1, 0)])


def per_device(routes, gates, hidden, w_down, out_grad):
    experts = lax.axis_size("expert")
    n_dp = lax.axis_size("dp")
    dp = lax.axis_index("dp")
    h_local = hidden[0]
    w_local = w_down[0]
    slots, part = h_local.shape
    cap = slots // experts
    width = w_local.shape[1]
    tok = routes.shape[0]
    large = experts * tok > 4096
    chunks = 4 if large else CHUNKS
    step = width // chunks

    named = routes[None] == jnp.arange(experts, dtype=jnp.int32)[:, None, None]
    dense = jnp.max(jnp.where(named, gates[None], jnp.float32(-1.0)), axis=2)
    mine = lax.all_to_all(dense, "expert", split_axis=0, concat_axis=0, tiled=True)
    taken = mine >= 0
    earlier = (jnp.arange(tok)[:, None] < jnp.arange(tok)[None, :]).astype(jnp.bfloat16)
    rank = jnp.dot(taken.astype(jnp.bfloat16), earlier, preferred_element_type=jnp.float32)
    rank = jnp.where(taken, rank, -1.0).astype(jnp.int32)
    pick = rank[:, None, :] == jnp.arange(cap, dtype=jnp.int32)[None, :, None]
    slot_gate = jnp.sum(jnp.where(pick, mine[:, None, :], 0.0), axis=2)[:, :, None]
    sel = pick.astype(jnp.bfloat16)

    if n_dp == 2:
        other = swap(h_local)
        whole = jnp.where(
            dp == 0,
            jnp.concatenate([h_local, other], axis=1),
            jnp.concatenate([other, h_local], axis=1),
        )
    else:
        whole = lax.all_gather(h_local, "dp", axis=1, tiled=True)

    mixed, weight_grad = [], []
    partial_hidden = jnp.zeros((slots, whole.shape[1]), jnp.float32)
    dots = jnp.zeros((experts, cap), jnp.float32)
    for c in range(chunks):
        grad_c = out_grad[:, c * step : (c + 1) * step]
        w_c = w_local[:, c * step : (c + 1) * step]
        if large and c:
            grad_c, w_c, partial_hidden, dots, mixed[-1] = lax.optimization_barrier(
                (grad_c, w_c, partial_hidden, dots, mixed[-1])
            )
        og = lax.all_gather(grad_c, "expert", axis=0, tiled=True).reshape(experts, tok, step)
        out = jnp.dot(whole, w_c, preferred_element_type=jnp.float32).astype(jnp.bfloat16)
        out = out.reshape(experts, cap, step)
        scaled = (slot_gate * out.astype(jnp.float32)).astype(jnp.bfloat16)
        share = jnp.einsum(
            "jrt,jrc->jtc", sel, scaled, preferred_element_type=jnp.float32
        ).astype(jnp.bfloat16)
        mixed.append(
            lax.psum_scatter(
                share.reshape(experts * tok, step), "expert", scatter_dimension=0, tiled=True
            )
        )
        rows = jnp.einsum(
            "jrt,jtc->jrc", sel, og, preferred_element_type=jnp.float32
        ).astype(jnp.bfloat16)
        rows = rows.astype(jnp.float32)
        dots = dots + jnp.sum(rows * out.astype(jnp.float32), axis=2)
        grad_slots = (slot_gate * rows).astype(jnp.bfloat16).reshape(slots, step)
        weight_grad.append(
            lax.dot_general(
                whole, grad_slots, (((0,), (0,)), ((), ())), preferred_element_type=jnp.float32
            ).astype(jnp.bfloat16)
        )
        partial_hidden = partial_hidden + lax.dot_general(
            grad_slots, w_c, (((1,), (1,)), ((), ())), preferred_element_type=jnp.float32
        )
    by_token = jnp.sum(jnp.where(pick, dots[:, :, None], 0.0), axis=1)
    back = lax.all_to_all(by_token, "expert", split_axis=0, concat_axis=0, tiled=True)
    gate_part = jnp.sum(jnp.where(named, back[:, :, None], 0.0), axis=0)
    rounded = partial_hidden.astype(jnp.bfloat16)
    if n_dp == 2:
        gate_grad = gate_part + swap(gate_part)
        keep = lax.dynamic_slice_in_dim(rounded, dp * part, part, axis=1)
        give = lax.dynamic_slice_in_dim(rounded, (1 - dp) * part, part, axis=1)
        hidden_grad = (keep.astype(jnp.float32) + swap(give).astype(jnp.float32)).astype(jnp.bfloat16)
    else:
        gate_grad = lax.psum(gate_part, "dp")
        hidden_grad = lax.psum_scatter(rounded, "dp", scatter_dimension=1, tiled=True)
    mixed = jnp.concatenate(mixed, axis=1)
    weight_grad = jnp.concatenate(weight_grad, axis=1)
    return (mixed, hidden_grad[None], weight_grad[None], gate_grad)


def solution(mesh):
    in_specs = (
        P("expert", None),
        P("expert", None),
        P("expert", None, "dp"),
        P("expert", None, "dp"),
        P("expert", "dp"),
    )
    out_specs = (
        P("expert", "dp"),
        P("expert", None, "dp"),
        P("expert", None, "dp"),
        P("expert", None),
    )
    return jax.shard_map(
        per_device, mesh=mesh, in_specs=in_specs, out_specs=out_specs, check_vma=False
    )
```

time: 495 us -> 360 us (0.73)
  waiting for transfers between devices: 343 us -> 220 us
  matrix products: 45.2 us -> 83.5 us
  local copies, waits for them, and re-layouts: 31.7 us -> 4.94 us
  other arithmetic: 39.7 us -> 20.9 us
  blocking collectives: 9.16 us -> 0 us
    all_to_all x2, waiting for transfers between devices: 301 us -> 3.98 us  [the longest x1 3.97 us: per_device(): lax.all_to_all(dense, 'expert', split_axis=0, concat_axis=0, tiled=True)]
    reduce_scatter x1 -> x2, waiting for transfers between devices: 0.01 us -> 117 us  [per_device(): lax.psum_scatter(share.reshape(experts * tok, step), 'expert', scatter_di...]
    all_gather x1 -> x2, waiting for transfers between devices: 41.6 us -> 81.1 us  [per_device(): lax.all_gather(grad_c, 'expert', axis=0, tiled=True)]
    dot_general x2 -> x9, matrix products: 30.3 us -> 65.4 us  [the longest x2 19.3 us: per_device(): jnp.dot(whole, w_c, preferred_element_type=jnp.float32).astype(jnp.bfloat16)]
    gather x1 -> x0, local copies, waits for them, and re-layouts: 18.6 us -> none  [per_device(): rows = jnp.take(returned.reshape(experts * cap, width), target, axis=0)]
    ppermute x0 -> x3, waiting for transfers between devices: none -> 17.6 us  [swap(): return lax.ppermute(x, 'dp', [(0, 1), (1, 0)])]
    reduce_sum x3 -> x2, other arithmetic: 18.1 us -> 0.88 us  [the longest x1 0.86 us: per_device(): by_token = jnp.sum(jnp.where(pick, dots[:, :, None], 0.0), axis=1)]
    scatter x1 -> x0, other arithmetic: 15.6 us -> none  [per_device(): jnp.zeros((experts * cap, width), jnp.bfloat16).at[target].set(send_grad)]
  transfers between devices with their start and end apart: 4 -> 9, of which waited for: 3 -> 6; matrix products, arithmetic and copies ran while one was open for 19% -> 25% of each run, Pallas kernels for 0% -> 0%
where the time goes in v1:
time: 360 us; the launch traced here: 358 us
  waiting for transfers between devices  220 us (61%)
  matrix products  83.5 us (23%)
  other arithmetic  20.9 us (6%)
  starting transfers between devices  14.8 us (4%)
  between operations  13.9 us (4%)
  local copies, waits for them, and re-layouts  4.94 us (1%)
    reduce_scatter x2, waiting for transfers between devices, per_device(): lax.psum_scatter(share.reshape(experts * tok, step), 'expert', scatter_di...  117 us
    all_gather x2, waiting for transfers between devices, per_device(): lax.all_gather(grad_c, 'expert', axis=0, tiled=True)  81.1 us
    dot_general x2, matrix products, per_device(): jnp.dot(whole, w_c, preferred_element_type=jnp.float32).astype(jnp.bfloat16)  19.3 us
    dot_general x2, matrix products, per_device(): lax.dot_general(whole, grad_slots, (((0,), (0,)), ((), ())), preferred_el...  18.1 us
    ppermute x3, waiting for transfers between devices, swap(): return lax.ppermute(x, 'dp', [(0, 1), (1, 0)])  17.6 us
    dot_general x2, matrix products, per_device(): lax.dot_general(grad_slots, w_c, (((1,), (1,)), ((), ())), preferred_elem...  17.4 us
    dot_general x2, matrix products, per_device(): jnp.einsum('jrt,jtc->jrc', sel, og, preferred_element_type=jnp.float32)  16 us
    dot_general x2, matrix products, per_device(): jnp.einsum('jrt,jrc->jtc', sel, scaled, preferred_element_type=jnp.float32)  12.5 us
  transfers between devices with their start and end apart: 9, of which 6 were waited for; matrix products, arithmetic and copies ran while one was open for 25% of the time, Pallas kernels for 0%

profile of v1, /device:TPU:16, one launch (start us, length us, event | category | flops | bytes accessed | tf_op | source)
XLA Modules:
  0.0 358.0 jit_solution(9271909161463053405)
XLA Ops:
  7.2 0.0 all-gather.3.cloned.1.call-start
  7.2 2.1 fusion.24
  9.3 0.0 all-gather.3.cloned.1.call-update
  9.4 0.0 all-gather.5.cloned.1.call-start
  9.4 0.7 all-gather.5.cloned.1.call-update
  10.1 1.6 collective-permute-start
  11.7 1.3 select_reduce_fusion.3
  13.0 6.2 %all-to-all-start = ((f32[16,1,128]{2,1,0:T(1,128)}), f32[16,1,128]{2,1,0:T(1,128)S(1)}, u32[]{:S(2)}, u32[]{:S(2)}) async-start(f32[16,1,128]{2,1,0:T(1,128)} %bitcast.1), calls=%async_computation | async-start | bytes 16384 | tf_op jit(solution)/shard_map/all_to_all | solution.py:29
  19.2 0.0 reduce-scatter.5.cloned.1.call-start
  19.2 4.0 %all-to-all-done = f32[16,1,128]{2,1,0:T(1,128)S(1)} async-done(((f32[16,1,128]{2,1,0:T(1,128)}), f32[16,1,128]{2,1,0:T(1,128)S(1)}, u32[]{:S(2)}, u32[]{:S(2)}) %all-to-all-start) | async-done | bytes 8224 | tf_op jit(solution)/shard_map/all_to_all | solution.py:29
  23.2 0.1 fusion.16
  23.4 17.6 %collective-permute-done = bf16[1280,512]{1,0:T(8,128)(2,1)S(1)} collective-permute-done((bf16[1280,512]{1,0:T(8,128)(2,1)}, bf16[1280,512]{1,0:T(8,128)(2,1)S(1)}, u32[]{:S(2)}, u32[]{:S(2)}) %collective-permute-start) | collective-permute-done | bytes 1310752 | tf_op jit(solution)/shard_map/ppermute | solution.py:10
  40.9 10.6 %convolution_convert_fusion = bf16[1280,1792]{1,0:T(8,128)(2,1)} fusion(bf16[1024,3584]{1,0:T(8,128)(2,1)} %bitcast.47, bf16[1280,512]{1,0:T(8,128)(2,1)S(1)} %collective-permute-done, bf16[1280,512]{1,0:T(8,128)(2,1)} %bitcast.52, pred[]{:T(512)S(6)} %eq.35), kind=kOutput, calls=%fused_computation.12 | convolution fusion | flops 4711710720 | bytes 10878977 | tf_op jit(solution)/shard_map/dot_general | solution.py:59
  51.5 0.0 copy-done.7
  51.5 8.7 %convolution_convert_fusion.1 = bf16[1280,1792]{1,0:T(8,128)(2,1)} fusion(bf16[1024,3584]{1,0:T(8,128)(2,1)} %bitcast.48, bf16[1280,512]{1,0:T(8,128)(2,1)S(1)} %collective-permute-done, bf16[1280,512]{1,0:T(8,128)(2,1)S(1)} %bitcast.54, pred[]{:T(512)S(6)} %eq.35), kind=kOutput, calls=%fused_computation.13 | convolution fusion | flops 4711710720 | bytes 10878977 | tf_op jit(solution)/shard_map/dot_general | solution.py:59
  60.2 19.4 %all-gather.3.cloned.1.call-done = bf16[2048,1792]{1,0:T(8,128)(2,1)} async-done(((bf16[128,1792]{1,0:T(8,128)(2,1)}), bf16[2048,1792]{1,0:T(8,128)(2,1)}) %all-gather.3.cloned.1.call-update) | async-done | bytes 7340048 | tf_op jit(solution)/shard_map/all_gather | solution.py:58
  79.6 7.9 %fusion.3 = (f32[16,80]{1,0:T(8,128)S(1)}, bf16[16,80,1792]{2,1,0:T(8,128)(2,1)}) fusion(bf16[16,80,1792]{2,1,0:T(8,128)(2,1)} %bitcast.30, bf16[16,128,1792]{2,1,0:T(8,128)(2,1)} %bitcast.36, s32[16,128]{1,0:T(8,128)S(1)} %fusion.16), kind=kOutput, calls=%fused_computation.9 | convolution fusion | flops 598833920 | bytes 16528384 | tf_op jit(solution)/shard_map/jrt,jtc->jrc/dot_general | solution.py:70
  87.5 61.7 %all-gather.5.cloned.1.call-done = bf16[2048,1792]{1,0:T(8,128)(2,1)} async-done(((bf16[128,1792]{1,0:T(8,128)(2,1)}), bf16[2048,1792]{1,0:T(8,128)(2,1)}) %all-gather.5.cloned.1.call-update) | async-done | bytes 7340048 | tf_op jit(solution)/shard_map/all_gather | solution.py:58
  149.2 8.1 %fusion.5 = (f32[16,80]{1,0:T(8,128)S(1)}, bf16[16,80,1792]{2,1,0:T(8,128)(2,1)}) fusion(bf16[16,80,1792]{2,1,0:T(8,128)(2,1)} %bitcast.32, bf16[16,128,1792]{2,1,0:T(8,128)(2,1)} %bitcast.37, s32[16,128]{1,0:T(8,128)S(1)} %fusion.16), kind=kOutput, calls=%fused_computation.11 | convolution fusion | flops 598833920 | bytes 16528384 | tf_op jit(solution)/shard_map/jrt,jtc->jrc/dot_general | solution.py:70
  157.3 0.9 select_reduce_fusion
  158.2 5.1 %convolution_convert_fusion.2 = bf16[16,128,1792]{2,1,0:T(8,128)(2,1)} fusion(bf16[16,80,1792]{2,1,0:T(8,128)(2,1)S(1)} %bitcast.35, f32[16,80]{1,0:T(8,128)S(1)} %get-tuple-element.5, s32[16,128]{1,0:T(8,128)S(1)} %fusion.16), kind=kOutput, calls=%fused_computation.15 | convolution fusion | flops 597917696 | bytes 11940864 | tf_op jit(solution)/shard_map/jrt,jrc->jtc/dot_general | solution.py:62
  163.3 0.0 reduce-scatter.5.cloned.1.call-update
  163.3 0.2 reduce-scatter.3.cloned.1.call-start
  163.5 7.4 %convolution_convert_fusion.3 = bf16[16,128,1792]{2,1,0:T(8,128)(2,1)} fusion(bf16[16,80,1792]{2,1,0:T(8,128)(2,1)} %bitcast.31, f32[16,80]{1,0:T(8,128)S(1)} %get-tuple-element.5, s32[16,128]{1,0:T(8,128)S(1)} %fusion.16), kind=kOutput, calls=%fused_computation.16 | convolution fusion | flops 597917696 | bytes 11940864 | tf_op jit(solution)/shard_map/jrt,jrc->jtc/dot_general | solution.py:62
  171.0 0.0 reduce-scatter.3.cloned.1.call-update
  171.0 7.5 %fusion.1 = (bf16[16,80,1792]{2,1,0:T(8,128)(2,1)S(1)}, bf16[16,80,1792]{2,1,0:T(8,128)(2,1)S(1)}) fusion(bf16[16,80,1792]{2,1,0:T(8,128)(2,1)} %get-tuple-element.13, f32[16,80]{1,0:T(8,128)S(1)} %get-tuple-element.5, bf16[16,80,1792]{2,1,0:T(8,128)(2,1)} %get-tuple-element.11), kind=kLoop, calls=%fused_computation.7 | loop fusion | flops 13762560 | bytes 18355200 | tf_op jit(solution)/shard_map/convert_element_type | solution.py:75
  178.5 0.0 copy-start
  178.5 0.0 copy-start.1
  178.5 10.2 %fusion.12 = f32[1280,1024]{1,0:T(8,128)S(1)} fusion(bf16[1280,1792]{1,0:T(8,128)(2,1)S(1)} %bitcast.38, bf16[1024,3584]{1,0:T(8,128)(2,1)} %bitcast.49), kind=kOutput, calls=%fused_computation.26 | convolution fusion | flops 4697620480 | bytes 13500416 | tf_op jit(solution)/shard_map/dot_general | solution.py:81
  188.7 7.2 %add_convert_fusion = bf16[1280,1024]{1,0:T(8,128)(2,1)S(1)} fusion(f32[1280,1024]{1,0:T(8,128)S(1)} %fusion.12, bf16[1280,1792]{1,0:T(8,128)(2,1)S(1)} %bitcast.42, bf16[1024,3584]{1,0:T(8,128)(2,1)} %bitcast.50), kind=kOutput, calls=%fused_computation.17 | convolution fusion | flops 4700241920 | bytes 16121856 | tf_op jit(solution)/shard_map/dot_general | solution.py:81
  196.0 1.6 copy-done.2
  197.6 1.2 constant_dynamic-slice_fusion
  198.8 1.5 collective-permute-start.1
  200.2 4.6 %all-to-all-start.1 = ((f32[16,1,128]{2,1,0:T(1,128)}), f32[16,1,128]{2,1,0:T(1,128)S(1)}, u32[]{:S(2)}, u32[]{:S(2)}) async-start(f32[16,1,128]{2,1,0:T(1,128)} %bitcast.17), calls=%async_computation.3 | async-start | bytes 16384 | tf_op jit(solution)/shard_map/all_to_all | solution.py:85
  204.8 0.0 copy-start.6
  204.8 11.1 %convolution_convert_fusion.6 = bf16[1024,1792]{1,0:T(8,128)(2,1)} fusion(bf16[1280,1792]{1,0:T(8,128)(2,1)} %bitcast.43, bf16[1280,512]{1,0:T(8,128)(2,1)} %copy-done.7, bf16[1280,512]{1,0:T(8,128)(2,1)} %bitcast.53, pred[]{:T(512)S(6)} %eq.35), kind=kOutput, calls=%fused_computation.22 | convolution fusion | flops 4711251968 | bytes 10878977 | tf_op jit(solution)/shard_map/dot_general | solution.py:77
  215.9 0.0 copy-start.4
  215.9 7.0 %convolution_convert_fusion.7 = bf16[1024,1792]{1,0:T(8,128)(2,1)} fusion(bf16[1280,1792]{1,0:T(8,128)(2,1)S(1)} %bitcast.41, bf16[1280,512]{1,0:T(8,128)(2,1)S(1)} %copy-done.8, bf16[1280,512]{1,0:T(8,128)(2,1)S(1)} %bitcast.55, pred[]{:T(512)S(6)} %eq.35), kind=kOutput, calls=%fused_computation.23 | convolution fusion | flops 4711251968 | bytes 10878977 | tf_op jit(solution)/shard_map/dot_general | solution.py:77
  222.9 0.0 all-to-all-done.1
  223.0 0.7 collective-permute-start.2
  223.6 6.9 %maximum_bitcast_fusion = bf16[1,1024,3584]{2,1,0:T(8,128)(2,1)} fusion(bf16[1024,1792]{1,0:T(8,128)(2,1)} %convolution_convert_fusion.6, bf16[1024,1792]{1,0:T(8,128)(2,1)} %convolution_convert_fusion.7), kind=kLoop, calls=%fused_computation.14 | loop fusion | flops 14680064 | bytes 14680064 | tf_op jit(solution)/shard_map/broadcast_in_dim | solution.py:98
  230.5 0.0 collective-permute-done.2
  230.5 0.6 add.31
  231.1 0.0 collective-permute-done.1
  231.1 1.6 fusion.15
  232.7 21.3 %reduce-scatter.5.cloned.1.call-done = bf16[128,1792]{1,0:T(8,128)(2,1)} async-done(((bf16[2048,1792]{1,0:T(8,128)(2,1)}), bf16[128,1792]{1,0:T(8,128)(2,1)}) %reduce-scatter.5.cloned.1.call-update) | async-done | bytes 458768 | tf_op jit(solution)/shard_map/reduce_scatter | solution.py:66
  254.0 95.3 %reduce-scatter.3.cloned.1.call-done = bf16[128,1792]{1,0:T(8,128)(2,1)} async-done(((bf16[2048,1792]{1,0:T(8,128)(2,1)}), bf16[128,1792]{1,0:T(8,128)(2,1)}) %reduce-scatter.3.cloned.1.call-update) | async-done | bytes 458768 | tf_op jit(solution)/shard_map/reduce_scatter | solution.py:66
  349.3 2.1 pad_maximum_fusion
  (24 shorter events, 0.1 us)
Async XLA Ops:
  7.2 72.5 %all-gather.3.cloned.1.call-start = ((), (), s32[]{:S(2)}) async-start(), calls=%async_computation.6 | async-start | bytes 7798784 | tf_op jit(solution)/shard_map/all_gather | solution.py:58
  9.4 139.8 %all-gather.5.cloned.1.call-start = ((), (), s32[]{:S(2)}) async-start(), calls=%async_computation.7 | async-start | bytes 7798784 | tf_op jit(solution)/shard_map/all_gather | solution.py:58
  10.1 30.8 %collective-permute-start = (bf16[1280,512]{1,0:T(8,128)(2,1)}, bf16[1280,512]{1,0:T(8,128)(2,1)S(1)}, u32[]{:S(2)}, u32[]{:S(2)}) collective-permute-start(bf16[1280,512]{1,0:T(8,128)(2,1)} %bitcast.51), channel_id=1, source_target_pairs={{0,16},{16,0},{1,17},{17,1},{2,18},{18,2},{3,19},{19,3},{4,20},{20... | collective-permute-start | bytes 3932168 | tf_op jit(solution)/shard_map/ppermute | solution.py:10
  13.0 10.2 %all-to-all-start = ((f32[16,1,128]{2,1,0:T(1,128)}), f32[16,1,128]{2,1,0:T(1,128)S(1)}, u32[]{:S(2)}, u32[]{:S(2)}) async-start(f32[16,1,128]{2,1,0:T(1,128)} %bitcast.1), calls=%async_computation | async-start | bytes 16384 | tf_op jit(solution)/shard_map/all_to_all | solution.py:29
  19.2 234.8 %reduce-scatter.5.cloned.1.call-start = ((), (), s32[]{:S(2)}) async-start(), calls=%async_computation.5 | async-start | bytes 7798784 | tf_op jit(solution)/shard_map/reduce_scatter | solution.py:66
  40.9 10.6 %copy-start.7 = (bf16[1280,512]{1,0:T(8,128)(2,1)}, bf16[1280,512]{1,0:T(8,128)(2,1)S(1)}, u32[]{:S(2)}) copy-start(bf16[1280,512]{1,0:T(8,128)(2,1)S(1)} %collective-permute-done) | copy-start | bytes 3932164
  40.9 10.6 %copy-start.5 = (bf16[1,1280,512]{2,1,0:T(8,128)(2,1)S(1)}, bf16[1,1280,512]{2,1,0:T(8,128)(2,1)}, u32[]{:S(2)}) copy-start(bf16[1,1280,512]{2,1,0:T(8,128)(2,1)} %param.7) | copy-start | bytes 3932164
  79.6 78.6 %slice-start = ((s8[4587520]{0:T(1024)(128)(4,1)}), s8[393216]{0:T(1024)(128)(4,1)S(1)}, s32[]{:S(2)}) async-start(s8[4587520]{0:T(1024)(128)(4,1)} %bitcast.33), calls=%async_computation.8 | async-start | bytes 786432
  149.2 9.0 %slice-start.1 = ((s8[4587520]{0:T(1024)(128)(4,1)}), s8[4194304]{0:T(1024)(128)(4,1)S(1)}, s32[]{:S(2)}) async-start(s8[4587520]{0:T(1024)(128)(4,1)} %bitcast.33), calls=%async_computation.9 | async-start | bytes 8388608
  163.3 186.0 %reduce-scatter.3.cloned.1.call-start = ((), (), s32[]{:S(2)}) async-start(), calls=%async_computation.4 | async-start | bytes 7798784 | tf_op jit(solution)/shard_map/reduce_scatter | solution.py:66
  178.5 10.2 %copy-start = (bf16[16,80,1792]{2,1,0:T(8,128)(2,1)}, bf16[16,80,1792]{2,1,0:T(8,128)(2,1)S(1)}, u32[]{:S(2)}) copy-start(bf16[16,80,1792]{2,1,0:T(8,128)(2,1)S(1)} %get-tuple-element.9) | copy-start | bytes 13762564
  178.5 10.2 %copy-start.1 = (bf16[16,80,1792]{2,1,0:T(8,128)(2,1)}, bf16[16,80,1792]{2,1,0:T(8,128)(2,1)S(1)}, u32[]{:S(2)}) copy-start(bf16[16,80,1792]{2,1,0:T(8,128)(2,1)S(1)} %get-tuple-element.8) | copy-start | bytes 13762564
  196.0 1.6 copy-start.2
  197.6 18.3 %slice-start.2 = ((s8[4587520]{0:T(1024)(128)(4,1)}), s8[393216]{0:T(1024)(128)(4,1)S(1)}, s32[]{:S(2)}) async-start(s8[4587520]{0:T(1024)(128)(4,1)} %bitcast.39), calls=%async_computation.10 | async-start | bytes 786432
  198.8 32.3 %collective-permute-start.1 = (bf16[1280,512]{1,0:T(8,128)(2,1)}, bf16[1280,512]{1,0:T(8,128)(2,1)S(1)}, u32[]{:S(2)}, u32[]{:S(2)}) collective-permute-start(bf16[1280,512]{1,0:T(8,128)(2,1)} %constant_dynamic-slice_fusion), channel_id=1, source_target_pairs={{0,16},{16,0},{1,17},{17,1},{2,18},{18,2},{3,19},{19,3},{4,20},{20... | collective-permute-start | bytes 3932168 | tf_op jit(solution)/shard_map/ppermute | solution.py:10
  200.2 22.7 %all-to-all-start.1 = ((f32[16,1,128]{2,1,0:T(1,128)}), f32[16,1,128]{2,1,0:T(1,128)S(1)}, u32[]{:S(2)}, u32[]{:S(2)}) async-start(f32[16,1,128]{2,1,0:T(1,128)} %bitcast.17), calls=%async_computation.3 | async-start | bytes 16384 | tf_op jit(solution)/shard_map/all_to_all | solution.py:85
  204.8 11.1 %slice-start.3 = ((s8[4587520]{0:T(1024)(128)(4,1)}), s8[4194304]{0:T(1024)(128)(4,1)S(1)}, s32[]{:S(2)}) async-start(s8[4587520]{0:T(1024)(128)(4,1)} %bitcast.39), calls=%async_computation.11 | async-start | bytes 8388608
  204.8 11.1 %copy-start.6 = (bf16[1,1280,512]{2,1,0:T(8,128)(2,1)S(1)}, bf16[1,1280,512]{2,1,0:T(8,128)(2,1)}, u32[]{:S(2)}) copy-start(bf16[1,1280,512]{2,1,0:T(8,128)(2,1)} %param.7) | copy-start | bytes 3932164
  204.8 11.1 %copy-start.8 = (bf16[1280,512]{1,0:T(8,128)(2,1)S(1)}, bf16[1280,512]{1,0:T(8,128)(2,1)}, u32[]{:S(2)}) copy-start(bf16[1280,512]{1,0:T(8,128)(2,1)} %copy-done.7) | copy-start | bytes 3932164
  215.9 7.0 %copy-start.4 = (s32[128,8]{0,1:T(8,128)S(1)}, s32[128,8]{0,1:T(8,128)}, u32[]{:S(2)}) copy-start(s32[128,8]{0,1:T(8,128)} %param.5) | copy-start | bytes 12292
  223.0 8.1 %copy-start.3 = (bf16[1280,1024]{1,0:T(8,128)(2,1)S(1)}, bf16[1280,1024]{1,0:T(8,128)(2,1)}, u32[]{:S(2)}) copy-start(bf16[1280,1024]{1,0:T(8,128)(2,1)} %copy-done.2) | copy-start | bytes 7864324
  223.0 7.5 %collective-permute-start.2 = (f32[128,8]{0,1:T(8,128)S(1)}, f32[128,8]{0,1:T(8,128)S(1)}, u32[]{:S(2)}, u32[]{:S(2)}) collective-permute-start(f32[128,8]{0,1:T(8,128)S(1)} %select_reduce_fusion.2), channel_id=1, source_target_pairs={{0,16},{16,0},{1,17},{17,1},{2,18},{18,2},{3,19},{19,3},{4,20},{20... | collective-permute-start | bytes 12296 | tf_op jit(solution)/shard_map/ppermute | solution.py:10
Sparse Core Ops, SparseCore 0:
  10.9 68.7 all-gather.2
  82.5 66.6 all-gather.4
  163.4 90.5 reduce-scatter.4
  257.9 91.3 reduce-scatter.2

commit v2 on v1

--- a/solution.py
+++ b/solution.py
@@ -8,6 +8,18 @@
 
 def swap(x):
     return lax.ppermute(x, "dp", [(0, 1), (1, 0)])
+
+
+def place(sel, rows):
+    return jnp.einsum(
+        "jrt,jrc->jtc", sel, rows, preferred_element_type=jnp.float32
+    ).astype(jnp.bfloat16)
+
+
+def take(sel, tokens):
+    return jnp.einsum(
+        "jrt,jtc->jrc", sel, tokens, preferred_element_type=jnp.float32
+    ).astype(jnp.bfloat16)
 
 
 def per_device(routes, gates, hidden, w_down, out_grad):
@@ -21,12 +33,35 @@
     width = w_local.shape[1]
     tok = routes.shape[0]
     large = experts * tok > 4096
+    paired = experts % 2 == 0 and not large
+    half = experts // 2
+    core = lax.axis_index("expert") % 2
+    across = [(i, i ^ 1) for i in range(experts)]
+    alike = [list(range(p, experts, 2)) for p in range(2)]
+
+    def own_first(x):
+        pairs = x.reshape((half, 2) + x.shape[1:])
+        even, odd = pairs[:, 0], pairs[:, 1]
+        return jnp.concatenate(
+            [jnp.where(core == 0, even, odd), jnp.where(core == 0, odd, even)], axis=0
+        )
+
+    def in_order(x):
+        own, other = x[:half], x[half:]
+        pairs = jnp.stack(
+            [jnp.where(core == 0, own, other), jnp.where(core == 0, other, own)], axis=1
+        )
+        return pairs.reshape(x.shape)
+
     chunks = 4 if large else CHUNKS
     step = width // chunks
 
     named = routes[None] == jnp.arange(experts, dtype=jnp.int32)[:, None, None]
     dense = jnp.max(jnp.where(named, gates[None], jnp.float32(-1.0)), axis=2)
     mine = lax.all_to_all(dense, "expert", split_axis=0, concat_axis=0, tiled=True)
+    if paired:
+        mine = own_first(mine)
+        h_local = own_first(h_local.reshape(experts, cap, part)).reshape(slots, part)
     taken = mine >= 0
     earlier = (jnp.arange(tok)[:, None] < jnp.arange(tok)[None, :]).astype(jnp.bfloat16)
     rank = jnp.dot(taken.astype(jnp.bfloat16), earlier, preferred_element_type=jnp.float32)
@@ -55,21 +90,35 @@
             grad_c, w_c, partial_hidden, dots, mixed[-1] = lax.optimization_barrier(
                 (grad_c, w_c, partial_hidden, dots, mixed[-1])
             )
-        og = lax.all_gather(grad_c, "expert", axis=0, tiled=True).reshape(experts, tok, step)
         out = jnp.dot(whole, w_c, preferred_element_type=jnp.float32).astype(jnp.bfloat16)
         out = out.reshape(experts, cap, step)
         scaled = (slot_gate * out.astype(jnp.float32)).astype(jnp.bfloat16)
-        share = jnp.einsum(
-            "jrt,jrc->jtc", sel, scaled, preferred_element_type=jnp.float32
-        ).astype(jnp.bfloat16)
-        mixed.append(
-            lax.psum_scatter(
-                share.reshape(experts * tok, step), "expert", scatter_dimension=0, tiled=True
+        if paired:
+            near = lax.all_gather(
+                grad_c, "expert", axis=0, tiled=True, axis_index_groups=alike
             )
-        )
-        rows = jnp.einsum(
-            "jrt,jtc->jrc", sel, og, preferred_element_type=jnp.float32
-        ).astype(jnp.bfloat16)
+            far = lax.ppermute(near, "expert", across)
+            give = place(sel[half:], scaled[half:])
+            got = lax.ppermute(give, "expert", across)
+            share = place(sel[:half], scaled[:half]).astype(jnp.float32) + got.astype(jnp.float32)
+            share = share.astype(jnp.bfloat16).reshape(half * tok, step)
+            mixed.append(
+                lax.psum_scatter(
+                    share, "expert", scatter_dimension=0, tiled=True, axis_index_groups=alike
+                )
+            )
+            rows = jnp.concatenate(
+                [
+                    take(sel[:half], near.reshape(half, tok, step)),
+                    take(sel[half:], far.reshape(half, tok, step)),
+                ],
+                axis=0,
+            )
+        else:
+            og = lax.all_gather(grad_c, "expert", axis=0, tiled=True)
+            share = place(sel, scaled).reshape(experts * tok, step)
+            mixed.append(lax.psum_scatter(share, "expert", scatter_dimension=0, tiled=True))
+            rows = take(sel, og.reshape(experts, tok, step))
         rows = rows.astype(jnp.float32)
         dots = dots + jnp.sum(rows * out.astype(jnp.float32), axis=2)
         grad_slots = (slot_gate * rows).astype(jnp.bfloat16).reshape(slots, step)
@@ -82,6 +131,8 @@
             grad_slots, w_c, (((1,), (1,)), ((), ())), preferred_element_type=jnp.float32
         )
     by_token = jnp.sum(jnp.where(pick, dots[:, :, None], 0.0), axis=1)
+    if paired:
+        by_token = in_order(by_token)
     back = lax.all_to_all(by_token, "expert", split_axis=0, concat_axis=0, tiled=True)
     gate_part = jnp.sum(jnp.where(named, back[:, :, None], 0.0), axis=0)
     rounded = partial_hidden.astype(jnp.bfloat16)
@@ -95,6 +146,8 @@
         hidden_grad = lax.psum_scatter(rounded, "dp", scatter_dimension=1, tiled=True)
     mixed = jnp.concatenate(mixed, axis=1)
     weight_grad = jnp.concatenate(weight_grad, axis=1)
+    if paired:
+        hidden_grad = in_order(hidden_grad.reshape(experts, cap, part)).reshape(slots, part)
     return (mixed, hidden_grad[None], weight_grad[None], gate_grad)
 
 

time: 360 us -> 398 us (1.11)
  waiting for transfers between devices: 220 us -> 253 us
  other arithmetic: 20.9 us -> 30.4 us
  matrix products: 83.5 us -> 76.9 us
    all_gather x2, waiting for transfers between devices: 81.1 us -> 136 us  [per_device(): lax.all_gather(grad_c, 'expert', axis=0, tiled=True, axis_index_groups=al...]
    reduce_scatter x2, waiting for transfers between devices: 117 us -> 84.8 us  [per_device(): lax.psum_scatter(share, 'expert', scatter_dimension=0, tiled=True, axis_i...]
    ppermute x0 -> x4, waiting for transfers between devices: none -> 12.9 us  [the longest x2 12.9 us: per_device(): got = lax.ppermute(give, 'expert', across)]
    convert_element_type x0 -> x2, other arithmetic: none -> 10.1 us  [the longest x1 9.54 us: per_device(): scaled = (slot_gate * out.astype(jnp.float32)).astype(jnp.bfloat16)]
    dot_general x4 -> x8, matrix products: 28.6 us -> 24 us  [the longest x4 14.7 us: place(): jnp.einsum('jrt,jrc->jtc', sel, rows, preferred_element_type=jnp.float32)]
    broadcast_in_dim x2 -> x1, other arithmetic: 8.46 us -> 7.01 us  [per_device(): return (mixed, hidden_grad[None], weight_grad[None], gate_grad)]
  transfers between devices with their start and end apart: 9 -> 13, of which waited for: 6 -> 8; matrix products, arithmetic and copies ran while one was open for 25% -> 19% of each run, Pallas kernels for 0% -> 0%
where the time goes in v2:
time: 398 us; the launch traced here: 396 us
  waiting for transfers between devices  253 us (64%)
  matrix products  76.9 us (19%)
  other arithmetic  30.4 us (8%)
  starting transfers between devices  14.7 us (4%)
  between operations  14.1 us (4%)
  local copies, waits for them, and re-layouts  6.46 us (2%)
    all_gather x2, waiting for transfers between devices, per_device(): lax.all_gather(grad_c, 'expert', axis=0, tiled=True, axis_index_groups=al...  136 us
    reduce_scatter x2, waiting for transfers between devices, per_device(): lax.psum_scatter(share, 'expert', scatter_dimension=0, tiled=True, axis_i...  84.8 us
    dot_general x2, matrix products, per_device(): lax.dot_general(whole, grad_slots, (((0,), (0,)), ((), ())), preferred_el...  18.2 us
    dot_general x2, matrix products, per_device(): jnp.dot(whole, w_c, preferred_element_type=jnp.float32).astype(jnp.bfloat16)  17.5 us
    dot_general x2, matrix products, per_device(): lax.dot_general(grad_slots, w_c, (((1,), (1,)), ((), ())), preferred_elem...  17.1 us
    ppermute x3, waiting for transfers between devices, swap(): return lax.ppermute(x, 'dp', [(0, 1), (1, 0)])  16.6 us
    dot_general x4, matrix products, place(): jnp.einsum('jrt,jrc->jtc', sel, rows, preferred_element_type=jnp.float32)  14.7 us
    ppermute x2, waiting for transfers between devices, per_device(): got = lax.ppermute(give, 'expert', across)  12.9 us
  transfers between devices with their start and end apart: 13, of which 8 were waited for; matrix products, arithmetic and copies ran while one was open for 19% of the time, Pallas kernels for 0%

profile of v2, /device:TPU:16, one launch (start us, length us, event | category | flops | bytes accessed | tf_op | source)
XLA Modules:
  0.0 395.7 jit_solution(5106846651828694188)
XLA Ops:
  7.2 2.2 fusion.29
  9.5 0.7 all-gather.5.cloned.1.call-update
  10.2 67.8 %all-gather.3.cloned.1.call-done = bf16[1024,1792]{1,0:T(8,128)(2,1)} async-done(((bf16[128,1792]{1,0:T(8,128)(2,1)}), bf16[1024,1792]{1,0:T(8,128)(2,1)}) %all-gather.3.cloned.1.call-update) | async-done | bytes 3670032 | tf_op jit(solution)/shard_map/all_gather | solution.py:97
  78.1 68.0 %all-gather.5.cloned.1.call-done = bf16[1024,1792]{1,0:T(8,128)(2,1)} async-done(((bf16[128,1792]{1,0:T(8,128)(2,1)}), bf16[1024,1792]{1,0:T(8,128)(2,1)}) %all-gather.5.cloned.1.call-update) | async-done | bytes 3670032 | tf_op jit(solution)/shard_map/all_gather | solution.py:97
  146.1 1.3 select_reduce_fusion.3
  147.4 4.5 %all-to-all-start = ((f32[16,1,128]{2,1,0:T(1,128)}), f32[16,1,128]{2,1,0:T(1,128)S(1)}, u32[]{:S(2)}, u32[]{:S(2)}) async-start(f32[16,1,128]{2,1,0:T(1,128)} %bitcast.1), calls=%async_computation | async-start | bytes 16384 | tf_op jit(solution)/shard_map/all_to_all | solution.py:61
  152.1 0.1 pad_maximum_fusion.2
  152.2 1.5 collective-permute-start
  153.8 2.2 all-to-all-done
  156.0 0.1 fusion.15
  156.1 2.9 convolution_convert_fusion.11
  159.1 0.2 copy-done.10
  159.3 0.8 convolution_convert_fusion.9
  160.0 2.8 convolution_convert_fusion.10
  162.8 2.8 convolution_convert_fusion.8
  165.6 0.8 pad_maximum_fusion
  166.5 16.6 %collective-permute-done = bf16[1280,512]{1,0:T(8,128)(2,1)S(1)} collective-permute-done((bf16[1280,512]{1,0:T(8,128)(2,1)S(1)}, bf16[1280,512]{1,0:T(8,128)(2,1)S(1)}, u32[]{:S(2)}, u32[]{:S(2)}) %collective-permute-start) | collective-permute-done | bytes 1310752 | tf_op jit(solution)/shard_map/ppermute | solution.py:10
  183.1 10.0 %fusion.1 = (f32[1280]{0:T(1024)S(1)}, f32[1280,1792]{1,0:T(8,128)}) fusion(bf16[16,80,1792]{2,1,0:T(8,128)(2,1)S(1)} %get-tuple-element.24, bf16[1024,3584]{1,0:T(8,128)(2,1)} %bitcast.86, bf16[1280,512]{1,0:T(8,128)(2,1)S(1)} %collective-permute-done, bf16[1280,512]{1,0:T(8,128)(2,1)S(1)} %bitcast.75, pred[]{:T(512)S(6)} %eq.48), kind=kOutput, calls=%fused_computation.5 | convolution fusion | flops 4720884736 | bytes 20059136 | tf_op jit(solution)/shard_map/dot_general | solution.py:93
  193.2 7.5 %fusion.3 = (f32[1280]{0:T(1024)S(1)}, f32[1280,1792]{1,0:T(8,128)}) fusion(bf16[16,80,1792]{2,1,0:T(8,128)(2,1)S(1)} %get-tuple-element.25, bf16[1024,3584]{1,0:T(8,128)(2,1)S(1)} %bitcast.91, bf16[1280,512]{1,0:T(8,128)(2,1)S(1)} %collective-permute-done, bf16[1280,512]{1,0:T(8,128)(2,1)S(1)} %bitcast.76, pred[]{:T(512)S(6)} %eq.48), kind=kOutput, calls=%fused_computation.7 | convolution fusion | flops 4720884736 | bytes 20059136 | tf_op jit(solution)/shard_map/dot_general | solution.py:93
  200.7 0.6 select_reduce_fusion
  201.3 9.5 %multiply_convert_fusion.1 = (bf16[16,80,1792]{2,1,0:T(8,128)(2,1)}, bf16[16,80,1792]{2,1,0:T(8,128)(2,1)S(1)}) fusion(f32[16,80,1792]{2,1,0:T(8,128)} %bitcast.64, f32[16,80]{1,0:T(8,128)S(1)} %get-tuple-element.5, f32[16,80,1792]{2,1,0:T(8,128)} %bitcast.65), kind=kLoop, calls=%fused_computation.9 | loop fusion | flops 9175040 | bytes 27530240 | tf_op jit(solution)/shard_map/convert_element_type | solution.py:95
  210.8 1.2 convolution_convert_fusion.2
  212.1 6.4 %collective-permute-done.2 = bf16[8,128,1792]{2,1,0:T(8,128)(2,1)S(1)} collective-permute-done((bf16[8,128,1792]{2,1,0:T(8,128)(2,1)S(1)}, bf16[8,128,1792]{2,1,0:T(8,128)(2,1)S(1)}, u32[]{:S(2)}, u32[]{:S(2)}) %collective-permute-start.2) | collective-permute-done | bytes 3670048 | tf_op jit(solution)/shard_map/ppermute | solution.py:102
  218.5 3.1 add_convert_fusion
  221.6 0.2 reduce-scatter.3.cloned.1.call-start
  221.8 4.6 %convolution_convert_fusion.4 = bf16[8,128,1792]{2,1,0:T(8,128)(2,1)} fusion(bf16[16,80,1792]{2,1,0:T(8,128)(2,1)} %get-tuple-element.14, s32[16,128]{1,0:T(8,128)S(1)} %fusion.15), kind=kOutput, calls=%fused_computation.22 | convolution fusion | flops 295600128 | bytes 5971968 | tf_op jit(solution)/shard_map/jrt,jrc->jtc/dot_general | solution.py:14
  226.5 0.1 collective-permute-start.1
  226.7 6.5 %collective-permute-done.1 = bf16[8,128,1792]{2,1,0:T(8,128)(2,1)} collective-permute-done((bf16[8,128,1792]{2,1,0:T(8,128)(2,1)}, bf16[8,128,1792]{2,1,0:T(8,128)(2,1)}, u32[]{:S(2)}, u32[]{:S(2)}) %collective-permute-start.1) | collective-permute-done | bytes 3670048 | tf_op jit(solution)/shard_map/ppermute | solution.py:102
  233.2 5.8 %add_convert_fusion.1 = bf16[8,128,1792]{2,1,0:T(8,128)(2,1)} fusion(bf16[8,128,1792]{2,1,0:T(8,128)(2,1)} %collective-permute-done.1, bf16[16,80,1792]{2,1,0:T(8,128)(2,1)} %get-tuple-element.14, s32[16,128]{1,0:T(8,128)S(1)} %fusion.15), kind=kOutput, calls=%fused_computation.16 | convolution fusion | flops 302940160 | bytes 9641984 | tf_op jit(solution)/shard_map/jrt,jrc->jtc/dot_general | solution.py:14
  239.0 6.7 %fusion.2 = (bf16[1280,1792]{1,0:T(8,128)(2,1)S(1)}, bf16[1280,1792]{1,0:T(8,128)(2,1)S(1)}) fusion(bf16[16,80,1792]{2,1,0:T(8,128)(2,1)} %copy-done.1, f32[1280]{0:T(1024)S(1)} %mul.49, bf16[16,80,1792]{2,1,0:T(8,128)(2,1)} %copy-done), kind=kLoop, calls=%fused_computation.6 | loop fusion | flops 13762560 | bytes 18355200 | tf_op jit(solution)/shard_map/convert_element_type | solution.py:124
  245.8 9.9 %fusion.8 = f32[1280,1024]{1,0:T(8,128)S(1)} fusion(bf16[1280,1792]{1,0:T(8,128)(2,1)S(1)} %get-tuple-element.13, bf16[1024,3584]{1,0:T(8,128)(2,1)} %bitcast.87), kind=kOutput, calls=%fused_computation.28 | convolution fusion | flops 4697620480 | bytes 13500416 | tf_op jit(solution)/shard_map/dot_general | solution.py:130
  255.7 7.3 %add_convert_fusion.2 = bf16[1280,1024]{1,0:T(8,128)(2,1)S(1)} fusion(f32[1280,1024]{1,0:T(8,128)S(1)} %fusion.8, bf16[1280,1792]{1,0:T(8,128)(2,1)S(1)} %get-tuple-element.12, bf16[1024,3584]{1,0:T(8,128)(2,1)} %bitcast.88), kind=kOutput, calls=%fused_computation.17 | convolution fusion | flops 4700241920 | bytes 16121856 | tf_op jit(solution)/shard_map/dot_general | solution.py:130
  263.0 1.5 copy-done.5
  264.5 1.2 constant_dynamic-slice_fusion
  265.7 1.5 collective-permute-start.5
  267.1 0.6 pad_maximum_fusion.6
  267.8 6.0 %all-to-all-start.1 = ((f32[16,1,128]{2,1,0:T(1,128)}), f32[16,1,128]{2,1,0:T(1,128)S(1)}, u32[]{:S(2)}, u32[]{:S(2)}) async-start(f32[16,1,128]{2,1,0:T(1,128)} %bitcast.32), calls=%async_computation.3 | async-start | bytes 16384 | tf_op jit(solution)/shard_map/all_to_all | solution.py:136
  273.8 11.3 %convolution_convert_fusion.6 = bf16[1024,1792]{1,0:T(8,128)(2,1)} fusion(bf16[1280,1792]{1,0:T(8,128)(2,1)} %copy-done.4, bf16[1280,512]{1,0:T(8,128)(2,1)} %copy-done.11, bf16[1280,512]{1,0:T(8,128)(2,1)} %bitcast.77, pred[]{:T(512)S(6)} %eq.48), kind=kOutput, calls=%fused_computation.24 | convolution fusion | flops 4711251968 | bytes 10878977 | tf_op jit(solution)/shard_map/dot_general | solution.py:126
  285.1 6.9 %convolution_convert_fusion.7 = bf16[1024,1792]{1,0:T(8,128)(2,1)} fusion(bf16[1280,1792]{1,0:T(8,128)(2,1)S(1)} %bitcast.69, bf16[1280,512]{1,0:T(8,128)(2,1)S(1)} %copy-done.12, bf16[1280,512]{1,0:T(8,128)(2,1)S(1)} %bitcast.78, pred[]{:T(512)S(6)} %eq.48), kind=kOutput, calls=%fused_computation.25 | convolution fusion | flops 4711251968 | bytes 10878977 | tf_op jit(solution)/shard_map/dot_general | solution.py:126
  292.1 0.6 collective-permute-start.6
  292.7 7.0 %maximum_bitcast_fusion = bf16[1,1024,3584]{2,1,0:T(8,128)(2,1)} fusion(bf16[1024,1792]{1,0:T(8,128)(2,1)} %convolution_convert_fusion.6, bf16[1024,1792]{1,0:T(8,128)(2,1)} %convolution_convert_fusion.7), kind=kLoop, calls=%fused_computation.14 | loop fusion | flops 14680064 | bytes 14680064 | tf_op jit(solution)/shard_map/broadcast_in_dim | solution.py:151
  299.7 0.6 add.48
  300.3 0.5 add_convert_fusion.3
  301.0 0.1 pad_maximum_fusion.3
  301.1 1.1 copy.44
  302.2 0.9 reduce-scatter.5.cloned.1.call-done
  303.1 83.9 %reduce-scatter.3.cloned.1.call-done = bf16[128,1792]{1,0:T(8,128)(2,1)} async-done(((bf16[1024,1792]{1,0:T(8,128)(2,1)}), bf16[128,1792]{1,0:T(8,128)(2,1)}) %reduce-scatter.3.cloned.1.call-update) | async-done | bytes 458768 | tf_op jit(solution)/shard_map/reduce_scatter | solution.py:106
  387.1 2.1 pad_maximum_fusion.4
  (59 shorter events, 0.8 us)
Async XLA Ops:
  7.2 144.8 %copy-start.2 = (bf16[1,1280,512]{2,1,0:T(8,128)(2,1)S(1)}, bf16[1,1280,512]{2,1,0:T(8,128)(2,1)}, u32[]{:S(2)}) copy-start(bf16[1,1280,512]{2,1,0:T(8,128)(2,1)} %param.7) | copy-start | bytes 3932164
  7.2 70.9 %all-gather.3.cloned.1.call-start = ((), (), s32[]{:S(2)}) async-start(), calls=%async_computation.6 | async-start | bytes 4128768 | tf_op jit(solution)/shard_map/all_gather | solution.py:97
  9.5 136.6 %all-gather.5.cloned.1.call-start = ((), (), s32[]{:S(2)}) async-start(), calls=%async_computation.7 | async-start | bytes 4128768 | tf_op jit(solution)/shard_map/all_gather | solution.py:97
  78.1 82.0 %collective-permute-start.3 = (bf16[1024,1792]{1,0:T(8,128)(2,1)}, bf16[1024,1792]{1,0:T(8,128)(2,1)}, u32[]{:S(2)}, u32[]{:S(2)}) collective-permute-start(bf16[1024,1792]{1,0:T(8,128)(2,1)} %all-gather.3.cloned.1.call-done), channel_id=1, source_target_pairs={{0,1},{1,0},{2,3},{3,2},{4,5},{5,4},{6,7},{7,6},{8,9},{9,8},{10,11... | collective-permute-start | bytes 11010056 | tf_op jit(solution)/shard_map/ppermute | solution.py:100
  146.1 16.7 %collective-permute-start.4 = (bf16[1024,1792]{1,0:T(8,128)(2,1)}, bf16[1024,1792]{1,0:T(8,128)(2,1)}, u32[]{:S(2)}, u32[]{:S(2)}) collective-permute-start(bf16[1024,1792]{1,0:T(8,128)(2,1)} %all-gather.5.cloned.1.call-done), channel_id=1, source_target_pairs={{0,1},{1,0},{2,3},{3,2},{4,5},{5,4},{6,7},{7,6},{8,9},{9,8},{10,11... | collective-permute-start | bytes 11010056 | tf_op jit(solution)/shard_map/ppermute | solution.py:100
  147.4 8.5 %all-to-all-start = ((f32[16,1,128]{2,1,0:T(1,128)}), f32[16,1,128]{2,1,0:T(1,128)S(1)}, u32[]{:S(2)}, u32[]{:S(2)}) async-start(f32[16,1,128]{2,1,0:T(1,128)} %bitcast.1), calls=%async_computation | async-start | bytes 16384 | tf_op jit(solution)/shard_map/all_to_all | solution.py:61
  151.9 151.3 %reduce-scatter.5.cloned.1.call-start = ((), (), s32[]{:S(2)}) async-start(), calls=%async_computation.5 | async-start | bytes 4128768 | tf_op jit(solution)/shard_map/reduce_scatter | solution.py:106
  152.2 40.9 %copy-start.7 = (bf16[16,80,512]{2,1,0:T(8,128)(2,1)}, bf16[16,80,512]{2,1,0:T(8,128)(2,1)S(1)}, u32[]{:S(2)}) copy-start(bf16[16,80,512]{2,1,0:T(8,128)(2,1)S(1)} %pad_maximum_fusion.2) | copy-start | bytes 3932164
  152.2 30.9 %collective-permute-start = (bf16[1280,512]{1,0:T(8,128)(2,1)S(1)}, bf16[1280,512]{1,0:T(8,128)(2,1)S(1)}, u32[]{:S(2)}, u32[]{:S(2)}) collective-permute-start(bf16[1280,512]{1,0:T(8,128)(2,1)S(1)} %bitcast.74), channel_id=1, source_target_pairs={{0,16},{16,0},{1,17},{17,1},{2,18},{18,2},{3,19},{19,3},{4,20},{20... | collective-permute-start | bytes 3932168 | tf_op jit(solution)/shard_map/ppermute | solution.py:10
  156.1 3.1 copy-start.10
  165.6 27.5 %slice-start.2 = ((s8[7340032]{0:T(1024)(128)(4,1)}), s8[3145728]{0:T(1024)(128)(4,1)S(1)}, s32[]{:S(2)}) async-start(s8[7340032]{0:T(1024)(128)(4,1)} %bitcast.89), calls=%async_computation.10 | async-start | bytes 6291456
  166.5 26.6 %copy-start = (bf16[16,80,1792]{2,1,0:T(8,128)(2,1)}, bf16[16,80,1792]{2,1,0:T(8,128)(2,1)S(1)}, u32[]{:S(2)}) copy-start(bf16[16,80,1792]{2,1,0:T(8,128)(2,1)S(1)} %get-tuple-element.24) | copy-start | bytes 13762564
  166.5 26.6 %copy-start.1 = (bf16[16,80,1792]{2,1,0:T(8,128)(2,1)}, bf16[16,80,1792]{2,1,0:T(8,128)(2,1)S(1)}, u32[]{:S(2)}) copy-start(bf16[16,80,1792]{2,1,0:T(8,128)(2,1)S(1)} %get-tuple-element.25) | copy-start | bytes 13762564
  183.1 10.0 %copy-start.11 = (bf16[1280,512]{1,0:T(8,128)(2,1)}, bf16[1280,512]{1,0:T(8,128)(2,1)S(1)}, u32[]{:S(2)}) copy-start(bf16[1280,512]{1,0:T(8,128)(2,1)S(1)} %collective-permute-done) | copy-start | bytes 3932164
  183.1 10.0 %slice-start.3 = ((s8[7340032]{0:T(1024)(128)(4,1)}), s8[4194304]{0:T(1024)(128)(4,1)S(1)}, s32[]{:S(2)}) async-start(s8[7340032]{0:T(1024)(128)(4,1)} %bitcast.89), calls=%async_computation.11 | async-start | bytes 8388608
  212.0 6.5 %collective-permute-start.2 = (bf16[8,128,1792]{2,1,0:T(8,128)(2,1)S(1)}, bf16[8,128,1792]{2,1,0:T(8,128)(2,1)S(1)}, u32[]{:S(2)}, u32[]{:S(2)}) collective-permute-start(bf16[8,128,1792]{2,1,0:T(8,128)(2,1)S(1)} %convolution_convert_fusion.2), channel_id=1, source_target_pairs={{0,1},{1,0},{2,3},{3,2},{4,5},{5,4},{6,7},{7,6},{8,9},{9,8},{10,11... | collective-permute-start | bytes 11010056 | tf_op jit(solution)/shard_map/ppermute | solution.py:102
  221.6 165.4 %reduce-scatter.3.cloned.1.call-start = ((), (), s32[]{:S(2)}) async-start(), calls=%async_computation.4 | async-start | bytes 4128768 | tf_op jit(solution)/shard_map/reduce_scatter | solution.py:106
  226.5 6.8 %collective-permute-start.1 = (bf16[8,128,1792]{2,1,0:T(8,128)(2,1)}, bf16[8,128,1792]{2,1,0:T(8,128)(2,1)}, u32[]{:S(2)}, u32[]{:S(2)}) collective-permute-start(bf16[8,128,1792]{2,1,0:T(8,128)(2,1)} %convolution_convert_fusion.4), channel_id=1, source_target_pairs={{0,1},{1,0},{2,3},{3,2},{4,5},{5,4},{6,7},{7,6},{8,9},{9,8},{10,11... | collective-permute-start | bytes 11010056 | tf_op jit(solution)/shard_map/ppermute | solution.py:102
  245.8 9.9 %copy-start.3 = (bf16[1280,1792]{1,0:T(8,128)(2,1)}, bf16[1280,1792]{1,0:T(8,128)(2,1)S(1)}, u32[]{:S(2)}) copy-start(bf16[1280,1792]{1,0:T(8,128)(2,1)S(1)} %get-tuple-element.13) | copy-start | bytes 13762564
  245.8 9.9 %copy-start.4 = (bf16[1280,1792]{1,0:T(8,128)(2,1)}, bf16[1280,1792]{1,0:T(8,128)(2,1)S(1)}, u32[]{:S(2)}) copy-start(bf16[1280,1792]{1,0:T(8,128)(2,1)S(1)} %get-tuple-element.12) | copy-start | bytes 13762564
  263.0 1.5 copy-start.5
  264.5 20.7 %slice-start = ((s8[4587520]{0:T(1024)(128)(4,1)}), s8[393216]{0:T(1024)(128)(4,1)S(1)}, s32[]{:S(2)}) async-start(s8[4587520]{0:T(1024)(128)(4,1)} %bitcast.68), calls=%async_computation.8 | async-start | bytes 786432
  265.7 34.7 %collective-permute-start.5 = (bf16[1280,512]{1,0:T(8,128)(2,1)}, bf16[1280,512]{1,0:T(8,128)(2,1)S(1)}, u32[]{:S(2)}, u32[]{:S(2)}) collective-permute-start(bf16[1280,512]{1,0:T(8,128)(2,1)} %constant_dynamic-slice_fusion), channel_id=1, source_target_pairs={{0,16},{16,0},{1,17},{17,1},{2,18},{18,2},{3,19},{19,3},{4,20},{20... | collective-permute-start | bytes 3932168 | tf_op jit(solution)/shard_map/ppermute | solution.py:10
  267.8 24.3 %all-to-all-start.1 = ((f32[16,1,128]{2,1,0:T(1,128)}), f32[16,1,128]{2,1,0:T(1,128)S(1)}, u32[]{:S(2)}, u32[]{:S(2)}) async-start(f32[16,1,128]{2,1,0:T(1,128)} %bitcast.32), calls=%async_computation.3 | async-start | bytes 16384 | tf_op jit(solution)/shard_map/all_to_all | solution.py:136
  273.8 11.3 %slice-start.1 = ((s8[4587520]{0:T(1024)(128)(4,1)}), s8[4194304]{0:T(1024)(128)(4,1)S(1)}, s32[]{:S(2)}) async-start(s8[4587520]{0:T(1024)(128)(4,1)} %bitcast.68), calls=%async_computation.9 | async-start | bytes 8388608
  273.8 11.3 %copy-start.8 = (bf16[16,80,512]{2,1,0:T(8,128)(2,1)S(1)}, bf16[16,80,512]{2,1,0:T(8,128)(2,1)}, u32[]{:S(2)}) copy-start(bf16[16,80,512]{2,1,0:T(8,128)(2,1)} %copy-done.7) | copy-start | bytes 3932164
  273.8 11.3 %copy-start.12 = (bf16[1280,512]{1,0:T(8,128)(2,1)S(1)}, bf16[1280,512]{1,0:T(8,128)(2,1)}, u32[]{:S(2)}) copy-start(bf16[1280,512]{1,0:T(8,128)(2,1)} %copy-done.11) | copy-start | bytes 3932164
  285.1 7.0 %copy-start.9 = (s32[128,8]{0,1:T(8,128)S(1)}, s32[128,8]{0,1:T(8,128)}, u32[]{:S(2)}) copy-start(s32[128,8]{0,1:T(8,128)} %param.5) | copy-start | bytes 12292
  292.1 8.2 %copy-start.6 = (bf16[1280,1024]{1,0:T(8,128)(2,1)S(1)}, bf16[1280,1024]{1,0:T(8,128)(2,1)}, u32[]{:S(2)}) copy-start(bf16[1280,1024]{1,0:T(8,128)(2,1)} %copy-done.5) | copy-start | bytes 7864324
  292.1 7.6 %collective-permute-start.6 = (f32[128,8]{0,1:T(8,128)S(1)}, f32[128,8]{0,1:T(8,128)S(1)}, u32[]{:S(2)}, u32[]{:S(2)}) collective-permute-start(f32[128,8]{0,1:T(8,128)S(1)} %select_reduce_fusion.2), channel_id=1, source_target_pairs={{0,16},{16,0},{1,17},{17,1},{2,18},{18,2},{3,19},{19,3},{4,20},{20... | collective-permute-start | bytes 12296 | tf_op jit(solution)/shard_map/ppermute | solution.py:10
Sparse Core Ops, SparseCore 0:
  10.8 67.2 all-gather.2
  80.8 65.2 all-gather.4
  221.7 81.3 reduce-scatter.4
  306.6 80.3 reduce-scatter.2

commit v3 on v1

--- a/solution.py
+++ b/solution.py
@@ -3,7 +3,7 @@
 from jax import lax
 from jax.sharding import PartitionSpec as P
 
-CHUNKS = 2
+CHUNKS = 1
 
 
 def swap(x):

time: 360 us -> 303 us (0.84)
  waiting for transfers between devices: 220 us -> 182 us
  matrix products: 83.5 us -> 70.1 us
  local copies, waits for them, and re-layouts: 4.94 us -> 1.22 us
    reduce_scatter x2 -> x1, waiting for transfers between devices: 117 us -> 78.7 us  [per_device(): lax.psum_scatter(share.reshape(experts * tok, step), 'expert', scatter_di...]
    ppermute x3, waiting for transfers between devices: 17.6 us -> 29.3 us  [swap(): return lax.ppermute(x, 'dp', [(0, 1), (1, 0)])]
    all_gather x2 -> x1, waiting for transfers between devices: 81.1 us -> 69.6 us  [per_device(): lax.all_gather(grad_c, 'expert', axis=0, tiled=True)]
    broadcast_in_dim x2 -> x1, other arithmetic: 8.46 us -> 2.86 us  [per_device(): return (mixed, hidden_grad[None], weight_grad[None], gate_grad)]
    dot_general x2 -> x1, matrix products: 12.5 us -> 7.37 us  [per_device(): jnp.einsum('jrt,jrc->jtc', sel, scaled, preferred_element_type=jnp.float32)]
    convert_element_type x1, other arithmetic: 7.5 us -> 12.5 us  [per_device(): grad_slots = (slot_gate * rows).astype(jnp.bfloat16).reshape(slots, step)]
    dot_general x2 -> x1, matrix products: 19.3 us -> 16 us  [per_device(): jnp.dot(whole, w_c, preferred_element_type=jnp.float32).astype(jnp.bfloat16)]
    dot_general x2 -> x1, matrix products: 16 us -> 13.1 us  [per_device(): jnp.einsum('jrt,jtc->jrc', sel, og, preferred_element_type=jnp.float32)]
  transfers between devices with their start and end apart: 9 -> 7, of which waited for: 6 -> 5; matrix products, arithmetic and copies ran while one was open for 25% -> 23% of each run, Pallas kernels for 0% -> 0%
where the time goes in v3:
time: 303 us; the launch traced here: 301 us
  waiting for transfers between devices  182 us (60%)
  matrix products  70.1 us (23%)
  other arithmetic  18.2 us (6%)
  starting transfers between devices  14.6 us (5%)
  between operations  14.1 us (5%)
    reduce_scatter x1, waiting for transfers between devices, per_device(): lax.psum_scatter(share.reshape(experts * tok, step), 'expert', scatter_di...  78.7 us
    all_gather x1, waiting for transfers between devices, per_device(): lax.all_gather(grad_c, 'expert', axis=0, tiled=True)  69.6 us
    ppermute x3, waiting for transfers between devices, swap(): return lax.ppermute(x, 'dp', [(0, 1), (1, 0)])  29.3 us
    dot_general x1, matrix products, per_device(): lax.dot_general(whole, grad_slots, (((0,), (0,)), ((), ())), preferred_el...  17.3 us
    dot_general x1, matrix products, per_device(): lax.dot_general(grad_slots, w_c, (((1,), (1,)), ((), ())), preferred_elem...  16.2 us
    dot_general x1, matrix products, per_device(): jnp.dot(whole, w_c, preferred_element_type=jnp.float32).astype(jnp.bfloat16)  16 us
    dot_general x1, matrix products, per_device(): jnp.einsum('jrt,jtc->jrc', sel, og, preferred_element_type=jnp.float32)  13.1 us
    convert_element_type x1, other arithmetic, per_device(): grad_slots = (slot_gate * rows).astype(jnp.bfloat16).reshape(slots, step)  12.5 us
  transfers between devices with their start and end apart: 7, of which 5 were waited for; matrix products, arithmetic and copies ran while one was open for 23% of the time, Pallas kernels for 0%

profile of v3, /device:TPU:16, one launch (start us, length us, event | category | flops | bytes accessed | tf_op | source)
XLA Modules:
  0.0 300.6 jit_solution(14856710621498421382)
XLA Ops:
  7.2 0.0 all-gather.2.cloned.1.call-start
  7.2 0.7 all-gather.2.cloned.1.call-update
  7.9 1.6 collective-permute-start
  9.5 1.3 select_reduce_fusion.3
  10.8 6.2 %all-to-all-start = ((f32[16,1,128]{2,1,0:T(1,128)}), f32[16,1,128]{2,1,0:T(1,128)S(1)}, u32[]{:S(2)}, u32[]{:S(2)}) async-start(f32[16,1,128]{2,1,0:T(1,128)} %bitcast.1), calls=%async_computation | async-start | bytes 16384 | tf_op jit(solution)/shard_map/all_to_all | solution.py:29
  17.0 0.0 reduce-scatter.2.cloned.1.call-start
  17.0 4.0 %all-to-all-done = f32[16,1,128]{2,1,0:T(1,128)S(1)} async-done(((f32[16,1,128]{2,1,0:T(1,128)}), f32[16,1,128]{2,1,0:T(1,128)S(1)}, u32[]{:S(2)}, u32[]{:S(2)}) %all-to-all-start) | async-done | bytes 8224 | tf_op jit(solution)/shard_map/all_to_all | solution.py:29
  21.0 0.1 fusion.13
  21.1 17.6 %collective-permute-done = bf16[1280,512]{1,0:T(8,128)(2,1)S(1)} collective-permute-done((bf16[1280,512]{1,0:T(8,128)(2,1)}, bf16[1280,512]{1,0:T(8,128)(2,1)S(1)}, u32[]{:S(2)}, u32[]{:S(2)}) %collective-permute-start) | collective-permute-done | bytes 1310752 | tf_op jit(solution)/shard_map/ppermute | solution.py:10
  38.7 0.0 copy-start.1
  38.7 16.0 %convolution_convert_fusion = bf16[1280,3584]{1,0:T(8,128)(2,1)} fusion(bf16[1,1024,3584]{2,1,0:T(8,128)(2,1)} %param.8, bf16[1280,512]{1,0:T(8,128)(2,1)S(1)} %collective-permute-done, bf16[1280,512]{1,0:T(8,128)(2,1)} %bitcast.38, pred[]{:T(512)S(6)} %eq.35), kind=kOutput, calls=%fused_computation.6 | convolution fusion | flops 9411624960 | bytes 19136512 | tf_op jit(solution)/shard_map/dot_general | solution.py:59
  54.7 0.0 copy-done.1
  54.7 69.6 %all-gather.2.cloned.1.call-done = bf16[2048,3584]{1,0:T(8,128)(2,1)} async-done(((bf16[128,3584]{1,0:T(8,128)(2,1)}), bf16[2048,3584]{1,0:T(8,128)(2,1)}) %all-gather.2.cloned.1.call-update) | async-done | bytes 14680080 | tf_op jit(solution)/shard_map/all_gather | solution.py:58
  124.3 0.0 slice-start
  124.3 0.0 slice-start.1
  124.3 0.0 slice-start.2
  124.3 13.1 %fusion.2 = (f32[16,80]{1,0:T(8,128)S(1)}, bf16[16,80,3584]{2,1,0:T(8,128)(2,1)}) fusion(bf16[16,80,3584]{2,1,0:T(8,128)(2,1)} %bitcast.27, bf16[16,128,3584]{2,1,0:T(8,128)(2,1)} %bitcast.31, s32[16,128]{1,0:T(8,128)S(1)} %fusion.13), kind=kOutput, calls=%fused_computation.5 | convolution fusion | flops 1197505280 | bytes 33043456 | tf_op jit(solution)/shard_map/jrt,jtc->jrc/dot_general | solution.py:70
  137.5 0.9 select_reduce_fusion
  138.3 0.0 slice-done
  138.3 0.0 slice-done.1
  138.4 0.0 slice-done.2
  138.4 7.4 %convolution_convert_fusion.1 = bf16[16,128,3584]{2,1,0:T(8,128)(2,1)} fusion(bf16[16,80,3584]{2,1,0:T(8,128)(2,1)S(1)} %bitcast.30, f32[16,80]{1,0:T(8,128)S(1)} %get-tuple-element.5, s32[16,128]{1,0:T(8,128)S(1)} %fusion.13), kind=kOutput, calls=%fused_computation.7 | convolution fusion | flops 1195671552 | bytes 23868416 | tf_op jit(solution)/shard_map/jrt,jrc->jtc/dot_general | solution.py:62
  145.7 0.0 reduce-scatter.2.cloned.1.call-update
  145.8 4.7 %all-to-all-start.1 = ((f32[16,1,128]{2,1,0:T(1,128)}), f32[16,1,128]{2,1,0:T(1,128)S(1)}, u32[]{:S(2)}, u32[]{:S(2)}) async-start(f32[16,1,128]{2,1,0:T(1,128)} %bitcast.12), calls=%async_computation.2 | async-start | bytes 16384 | tf_op jit(solution)/shard_map/all_to_all | solution.py:85
  150.5 12.5 %fusion = bf16[16,80,3584]{2,1,0:T(8,128)(2,1)} fusion(bf16[16,80,3584]{2,1,0:T(8,128)(2,1)} %get-tuple-element.7, f32[16,80]{1,0:T(8,128)S(1)} %get-tuple-element.5), kind=kLoop, calls=%fused_computation.3 | loop fusion | flops 13762560 | bytes 18355200 | tf_op jit(solution)/shard_map/convert_element_type | solution.py:75
  163.0 0.0 copy-start
  163.0 16.2 %fusion.9 = bf16[1280,1024]{1,0:T(8,128)(2,1)S(1)} fusion(bf16[1280,3584]{1,0:T(8,128)(2,1)} %bitcast.32, bf16[1,1024,3584]{2,1,0:T(8,128)(2,1)} %param.8), kind=kOutput, calls=%fused_computation.15 | convolution fusion | flops 9396551680 | bytes 19136512 | tf_op jit(solution)/shard_map/dot_general | solution.py:81
  179.2 1.2 constant_dynamic-slice_fusion
  180.4 1.5 collective-permute-start.1
  181.9 0.0 all-to-all-done.1
  181.9 0.0 copy-done
  181.9 0.6 collective-permute-start.2
  182.6 17.3 %fusion.8 = bf16[1,1024,3584]{2,1,0:T(8,128)(2,1)} fusion(bf16[1280,3584]{1,0:T(8,128)(2,1)} %bitcast.33, bf16[1280,512]{1,0:T(8,128)(2,1)} %copy-done.1, bf16[1280,512]{1,0:T(8,128)(2,1)} %bitcast.39, pred[]{:T(512)S(6)} %eq.35), kind=kOutput, calls=%fused_computation.14 | convolution fusion | flops 9410707456 | bytes 19136512 | tf_op jit(solution)/shard_map/dot_general | solution.py:77
  199.8 11.8 %collective-permute-done.2 = f32[128,8]{0,1:T(8,128)S(1)} collective-permute-done((f32[128,8]{0,1:T(8,128)S(1)}, f32[128,8]{0,1:T(8,128)S(1)}, u32[]{:S(2)}, u32[]{:S(2)}) %collective-permute-start.2) | collective-permute-done | bytes 4128 | tf_op jit(solution)/shard_map/ppermute | solution.py:10
  211.6 0.6 add.17
  212.2 0.0 collective-permute-done.1
  212.2 2.9 fusion.12
  215.1 78.7 %reduce-scatter.2.cloned.1.call-done = bf16[128,3584]{1,0:T(8,128)(2,1)} async-done(((bf16[2048,3584]{1,0:T(8,128)(2,1)}), bf16[128,3584]{1,0:T(8,128)(2,1)}) %reduce-scatter.2.cloned.1.call-update) | async-done | bytes 917520 | tf_op jit(solution)/shard_map/reduce_scatter | solution.py:66
  (2 shorter events, 0.0 us)
Async XLA Ops:
  7.2 117.2 %all-gather.2.cloned.1.call-start = ((), (), s32[]{:S(2)}) async-start(), calls=%async_computation.4 | async-start | bytes 15597568 | tf_op jit(solution)/shard_map/all_gather | solution.py:58
  7.9 30.8 %collective-permute-start = (bf16[1280,512]{1,0:T(8,128)(2,1)}, bf16[1280,512]{1,0:T(8,128)(2,1)S(1)}, u32[]{:S(2)}, u32[]{:S(2)}) collective-permute-start(bf16[1280,512]{1,0:T(8,128)(2,1)} %bitcast.37), channel_id=1, source_target_pairs={{0,16},{16,0},{1,17},{17,1},{2,18},{18,2},{3,19},{19,3},{4,20},{20... | collective-permute-start | bytes 3932168 | tf_op jit(solution)/shard_map/ppermute | solution.py:10
  10.8 10.2 %all-to-all-start = ((f32[16,1,128]{2,1,0:T(1,128)}), f32[16,1,128]{2,1,0:T(1,128)S(1)}, u32[]{:S(2)}, u32[]{:S(2)}) async-start(f32[16,1,128]{2,1,0:T(1,128)} %bitcast.1), calls=%async_computation | async-start | bytes 16384 | tf_op jit(solution)/shard_map/all_to_all | solution.py:29
  17.0 276.8 %reduce-scatter.2.cloned.1.call-start = ((), (), s32[]{:S(2)}) async-start(), calls=%async_computation.3 | async-start | bytes 15597568 | tf_op jit(solution)/shard_map/reduce_scatter | solution.py:66
  38.7 16.0 %copy-start.1 = (bf16[1280,512]{1,0:T(8,128)(2,1)}, bf16[1280,512]{1,0:T(8,128)(2,1)S(1)}, u32[]{:S(2)}) copy-start(bf16[1280,512]{1,0:T(8,128)(2,1)S(1)} %collective-permute-done) | copy-start | bytes 3932164
  124.3 14.0 %slice-start = ((s8[9175040]{0:T(1024)(128)(4,1)}), s8[4194304]{0:T(1024)(128)(4,1)S(1)}, s32[]{:S(2)}) async-start(s8[9175040]{0:T(1024)(128)(4,1)} %bitcast.28), calls=%async_computation.5 | async-start | bytes 8388608
  124.3 14.0 %slice-start.1 = ((s8[9175040]{0:T(1024)(128)(4,1)}), s8[4194304]{0:T(1024)(128)(4,1)S(1)}, s32[]{:S(2)}) async-start(s8[9175040]{0:T(1024)(128)(4,1)} %bitcast.28), calls=%async_computation.6 | async-start | bytes 8388608
  124.3 14.0 %slice-start.2 = ((s8[9175040]{0:T(1024)(128)(4,1)}), s8[786432]{0:T(1024)(128)(4,1)S(1)}, s32[]{:S(2)}) async-start(s8[9175040]{0:T(1024)(128)(4,1)} %bitcast.28), calls=%async_computation.7 | async-start | bytes 1572864
  145.8 36.2 %all-to-all-start.1 = ((f32[16,1,128]{2,1,0:T(1,128)}), f32[16,1,128]{2,1,0:T(1,128)S(1)}, u32[]{:S(2)}, u32[]{:S(2)}) async-start(f32[16,1,128]{2,1,0:T(1,128)} %bitcast.12), calls=%async_computation.2 | async-start | bytes 16384 | tf_op jit(solution)/shard_map/all_to_all | solution.py:85
  163.0 18.9 %copy-start = (s32[128,8]{0,1:T(8,128)S(1)}, s32[128,8]{0,1:T(8,128)}, u32[]{:S(2)}) copy-start(s32[128,8]{0,1:T(8,128)} %param.5) | copy-start | bytes 12292
  180.4 31.8 %collective-permute-start.1 = (bf16[1280,512]{1,0:T(8,128)(2,1)}, bf16[1280,512]{1,0:T(8,128)(2,1)}, u32[]{:S(2)}, u32[]{:S(2)}) collective-permute-start(bf16[1280,512]{1,0:T(8,128)(2,1)} %constant_dynamic-slice_fusion), channel_id=1, source_target_pairs={{0,16},{16,0},{1,17},{17,1},{2,18},{18,2},{3,19},{19,3},{4,20},{20... | collective-permute-start | bytes 3932168 | tf_op jit(solution)/shard_map/ppermute | solution.py:10
  181.9 29.7 %collective-permute-start.2 = (f32[128,8]{0,1:T(8,128)S(1)}, f32[128,8]{0,1:T(8,128)S(1)}, u32[]{:S(2)}, u32[]{:S(2)}) collective-permute-start(f32[128,8]{0,1:T(8,128)S(1)} %select_reduce_fusion.2), channel_id=1, source_target_pairs={{0,16},{16,0},{1,17},{17,1},{2,18},{18,2},{3,19},{19,3},{4,20},{20... | collective-permute-start | bytes 12296 | tf_op jit(solution)/shard_map/ppermute | solution.py:10
Sparse Core Ops, SparseCore 0:
  10.3 114.0 all-gather.1
  145.9 147.8 reduce-scatter.1
